TPU v7x, 1024 devices: a whole 4x8x16 slice. The times are simulated.
1024 devices in a mesh: node: 64 (over y, x, core), local: 16 (over z).
Axes of the slice: x: 4, y: 8, z: 16, core: 2. Of those that a mesh axis runs over, the one named last changes fastest.
Arguments:
- tokens: bfloat16 [2048, 7168], P('node', 'local'), may hold values from -6 to 6
- cotangent: bfloat16 [2048, 7168], P('node', 'local'), may hold values from -1.5 to 1.5
- routes: int32 [2048, 8], P('node'), may hold values from 0 to 63, all different within a row; in each aligned block of 32 rows (0 to 31, 32 to 63, ...) at most 8 rows name the same one
- gate_probs: float32 [2048, 8], P('node'), may hold values from 0.1 to 1
- w_in: bfloat16 [64, 7168, 1024], P('node', 'local'), may hold values from -0.0625 to 0.0625
- w_out: bfloat16 [64, 1024, 7168], P('node', None, 'local'), may hold values from -0.1875 to 0.1875
Outputs:
- mixed: bfloat16 [2048, 7168], P('node', 'local')
- d_tokens: bfloat16 [2048, 7168], P('node', 'local')
- d_gates: float32 [2048, 8], P('node')
Inputs may be any that keep to these rules, and one draw needn't show every extreme that they name: `routes`: each row names 8 different experts. In each block of 32 rows (rows 0 to 31, and so on), no expert is named by more than 8 rows, a bound that some block reaches.
All inputs are finite; a program needn't handle non-finite values.
Results may differ from a plain program's by a relative error of at most 0.03.
Values may be sent and summed in bfloat16 or wider, within the bound.
No kernel may reach another device: no remote copies, remote signals or barrier semaphores. Data moves between devices by JAX's collectives and lax.ppermute only.
A program may use at most 32 MiB of HBM per device.

v0:
```python
import functools

import jax
import jax.numpy as jnp
from jax import lax
from jax.experimental import pallas as pl
from jax.experimental.pallas import tpu as pltpu
from jax.sharding import PartitionSpec as P

BF16 = jnp.bfloat16
F32 = jnp.float32
VMEM = pl.BlockSpec(memory_space=pltpu.VMEM)
HBM = pl.BlockSpec(memory_space=pltpu.HBM)
LARGE = 60 * 1024 * 1024
SMALL = 16 * 1024 * 1024


def pieces(rows, cols):
    half = cols // 2
    out = []
    for r in range(0, rows, 32):
        out.append((r, 32, 0, half))
        out.append((r, 32, half, half))
    r, nr, c, nc = out.pop()
    out.append((r, nr, c, nc // 2))
    out.append((r, nr, c + nc // 2, nc // 2))
    return out


def slot_columns(routes, node_count, capacity):
    tok, top = routes.shape
    rows = node_count * capacity
    expert = lax.broadcasted_iota(jnp.int32, (tok, node_count), 1)
    hits = jnp.zeros((tok, node_count), F32)
    for k in range(top):
        hits += jnp.where(routes[:, k : k + 1] == expert, 1.0, 0.0)
    earlier = lax.broadcasted_iota(jnp.int32, (tok, tok), 1) < lax.broadcasted_iota(jnp.int32, (tok, tok), 0)
    before = jnp.dot(jnp.where(earlier, 1.0, 0.0).astype(BF16), hits.astype(BF16), preferred_element_type=F32)
    col = lax.broadcasted_iota(jnp.int32, (tok, rows), 1)
    spread = jnp.where(
        lax.broadcasted_iota(jnp.int32, (node_count, rows), 1) // capacity
        == lax.broadcasted_iota(jnp.int32, (node_count, rows), 0),
        1.0,
        0.0,
    ).astype(BF16)
    before_cols = jnp.dot(before.astype(BF16), spread, preferred_element_type=F32)
    in_slot = before_cols == (col % capacity).astype(F32)
    return col // capacity, in_slot


def pack_kernel(node_count, capacity, routes_ref, tokens_ref, cot_ref, sent_ref):
    routes = routes_ref[...]
    expert, in_slot = slot_columns(routes, node_count, capacity)
    chosen = jnp.zeros(expert.shape, F32)
    for k in range(routes.shape[1]):
        chosen += jnp.where((routes[:, k : k + 1] == expert) & in_slot, 1.0, 0.0)
    chosen = chosen.T.astype(BF16)
    both = jnp.concatenate([tokens_ref[...].astype(F32), cot_ref[...].astype(F32)], axis=1).astype(BF16)
    sent_ref[...] = jnp.dot(chosen, both, preferred_element_type=F32).astype(BF16)


def terms_kernel(parts, x_ref, w_in_ref, w_out_ref, *refs):
    count = len(parts)
    outs, (pre_ref, dact_ref, sems) = refs[: 2 * count], refs[2 * count :]
    feat = w_in_ref.shape[0]
    rows = x_ref.shape[0]
    step = min(128, rows)
    copies = []
    for r0 in range(0, rows, step):
        band = slice(r0, r0 + step)
        pre_ref[band] = jnp.dot(x_ref[band, :feat], w_in_ref[...], preferred_element_type=F32).astype(BF16)
        dact_ref[band] = jnp.dot(x_ref[band, feat:], w_out_ref[...], preferred_element_type=F32).astype(BF16)
        for first, source in ((0, pre_ref), (count, dact_ref)):
            for i, (r, nr, c, nc) in enumerate(parts):
                if r0 <= r < r0 + step:
                    copy = pltpu.make_async_copy(
                        source.at[pl.ds(r, nr), pl.ds(c, nc)], outs[first + i], sems.at[first + i]
                    )
                    copy.start()
                    copies.append(copy)
    for copy in copies:
        copy.wait()


def outputs_kernel(parts, *refs):
    count = len(parts)
    sums = refs[: 2 * count]
    w_in_ref, w_out_ref, back_ref, pre_ref, dact_ref, sems = refs[2 * count :]
    feat = w_in_ref.shape[0]
    rows, width = back_ref.shape
    half = width // 2
    step = min(128, rows)
    copies = []
    for i, (r, nr, c, nc) in enumerate(parts):
        for first, target in ((0, pre_ref), (count, dact_ref)):
            copy = pltpu.make_async_copy(sums[first + i], target.at[pl.ds(r, nr), pl.ds(c, nc)], sems.at[first + i])
            copy.start()
            copies.append((r, copy))

    for r0 in range(0, rows, step):
        for r, copy in copies:
            if r0 <= r < r0 + step:
                copy.wait()
        band = slice(r0, r0 + step)
        pre = pre_ref[band].astype(F32)
        dact = dact_ref[band].astype(F32)
        sig = 1.0 / (1.0 + jnp.exp(-pre))
        act = (pre * sig).astype(BF16)
        dpre = (dact * sig * (1.0 + pre * (1.0 - sig))).astype(BF16)
        inner = jnp.sum(act.astype(F32) * dact, axis=1, keepdims=True)
        hi = inner.astype(BF16).astype(F32)
        mid = (inner - hi).astype(BF16).astype(F32)
        lo = inner - hi - mid
        y = lax.dot_general(act, w_out_ref[...], (((1,), (1,)), ((), ())), preferred_element_type=F32)
        dout = lax.dot_general(dpre, w_in_ref[...], (((1,), (1,)), ((), ())), preferred_element_type=F32)
        lane = lax.broadcasted_iota(jnp.int32, (step, half - feat), 1)
        extra = jnp.where(lane == 0, hi, jnp.where(lane == 1, mid, jnp.where(lane == 2, lo, 0.0)))
        back_ref[band, :feat] = y.astype(BF16)
        back_ref[band, feat:half] = extra.astype(BF16)
        back_ref[band, half : half + feat] = dout.astype(BF16)
        back_ref[band, half + feat :] = jnp.zeros((step, half - feat), BF16)


def unpack_kernel(node_count, capacity, routes_ref, gates_ref, back_ref, mixed_ref, d_tokens_ref, d_gates_ref):
    routes = routes_ref[...]
    gates = gates_ref[...]
    tok, top = routes.shape
    feat = mixed_ref.shape[1]
    half = back_ref.shape[1] // 2
    expert, in_slot = slot_columns(routes, node_count, capacity)
    weight = jnp.zeros(expert.shape, F32)
    picks = []
    for k in range(top):
        mine = (routes[:, k : k + 1] == expert) & in_slot
        weight += jnp.where(mine, gates[:, k : k + 1], 0.0)
        picks.append(jnp.where(mine, 1.0, 0.0).astype(BF16))
    hi = weight.astype(BF16)
    rest = weight - hi.astype(F32)
    mid = rest.astype(BF16)
    lo = (rest - mid.astype(F32)).astype(BF16)
    stack = jnp.concatenate([hi, mid, lo], axis=0)
    out = jnp.dot(stack, back_ref[...], preferred_element_type=F32)
    out = out[:tok] + (out[tok : 2 * tok] + out[2 * tok :])
    mixed_ref[...] = out[:, :feat].astype(BF16)
    d_tokens_ref[...] = out[:, half : half + feat].astype(BF16)
    tail = half - 128
    lane = lax.broadcasted_iota(jnp.int32, (1, 128), 1)
    column = lax.broadcasted_iota(jnp.int32, (tok, top), 1)
    d_gates = jnp.zeros((tok, top), F32)
    for k in range(top):
        got = jnp.dot(picks[k], back_ref[:, tail:half], preferred_element_type=F32)
        value = jnp.sum(jnp.where(lane >= feat - tail, got, 0.0), axis=1, keepdims=True)
        d_gates = jnp.where(column == k, value, d_gates)
    d_gates_ref[...] = d_gates


def call(kernel, in_specs, out_shape, out_space, *args, scratch=(), limit=SMALL):
    return pl.pallas_call(
        kernel,
        out_shape=out_shape,
        in_specs=in_specs,
        out_specs=jax.tree.map(lambda _: out_space, out_shape),
        scratch_shapes=scratch,
        compiler_params=pltpu.CompilerParams(vmem_limit_bytes=limit),
    )(*args)


def body(tokens, cotangent, routes, gate_probs, w_in, w_out):
    tok, feat = tokens.shape
    top = routes.shape[1]
    nodes = lax.axis_size("node")
    hidden = w_in.shape[2]
    capacity = min(tok, 2 * tok * top // nodes)
    rows = nodes * capacity
    width = 2 * (-(-(feat + 3) // 128) * 128)
    parts = pieces(rows, hidden)
    up, down = w_in[0], w_out[0].T
    scratch = [pltpu.VMEM((rows, hidden), BF16)] * 2 + [pltpu.SemaphoreType.DMA((2 * len(parts),))]

    def exchange(values):
        return lax.all_to_all(
            values.reshape(nodes, capacity, values.shape[1]), "node", split_axis=0, concat_axis=0, tiled=True
        ).reshape(rows, values.shape[1])

    sent = call(
        functools.partial(pack_kernel, nodes, capacity),
        [VMEM] * 3,
        jax.ShapeDtypeStruct((rows, 2 * feat), BF16),
        VMEM,
        routes,
        tokens,
        cotangent,
    )
    x_dy = exchange(sent)
    terms = call(
        functools.partial(terms_kernel, parts),
        [VMEM] * 3,
        tuple(jax.ShapeDtypeStruct((nr, nc), BF16) for _, nr, _, nc in parts) * 2,
        HBM,
        x_dy,
        up,
        down,
        scratch=scratch,
        limit=LARGE,
    )
    sums = lax.psum(tuple(terms), "local")
    back = call(
        functools.partial(outputs_kernel, parts),
        [HBM] * len(sums) + [VMEM] * 2,
        jax.ShapeDtypeStruct((rows, width), BF16),
        VMEM,
        *sums,
        up,
        down,
        scratch=scratch,
        limit=LARGE,
    )
    returned = exchange(back)
    return call(
        functools.partial(unpack_kernel, nodes, capacity),
        [VMEM] * 3,
        (
            jax.ShapeDtypeStruct((tok, feat), BF16),
            jax.ShapeDtypeStruct((tok, feat), BF16),
            jax.ShapeDtypeStruct((tok, top), F32),
        ),
        VMEM,
        routes,
        gate_probs,
        returned,
    )


def solution(mesh):
    in_specs = (
        P("node", "local"),
        P("node", "local"),
        P("node", None),
        P("node", None),
        P("node", "local", None),
        P("node", None, "local"),
    )
    out_specs = (P("node", "local"), P("node", "local"), P("node", None))
    return jax.shard_map(body, mesh=mesh, in_specs=in_specs, out_specs=out_specs, check_vma=False)
```

profile of v0, /device:TPU:1, one launch (start us, length us, event | category | flops | bytes accessed | tf_op | source)
XLA Modules:
  0.0 178.0 jit_solution(9447819624242806455)
XLA Ops:
  0.6 0.8 copy.10.routes_ref
  1.4 0.0 copy-start
  1.4 0.8 copy-done
  2.2 0.8 copy-done.1
  2.9 0.9 shard_map.85
  3.8 43.5 %all_to_all.10 = bf16[64,8,896]{2,1,0:T(8,128)(2,1)} all-to-all(bf16[64,8,896]{2,1,0:T(8,128)(2,1)S(1)} %bitcast.9), channel_id=1, replica_groups=mesh['node'=64,'local'=16] {'node'}, dimensions={0} | all-to-all | bytes 1835008 | tf_op jit(solution)/shard_map/all_to_all | solution.py:181
  47.3 4.3 %shard_map.86 = (bf16[32,512]{1,0:T(8,128)(2,1)}, bf16[32,512]{1,0:T(8,128)(2,1)}, bf16[32,512]{1,0:T(8,128)(2,1)}, bf16[32,512]{1,0:T(8,128)(2,1)}, bf16[32,512...) custom-call(bf16[512,896]{1,0:T(8,128)(2,1)} %bitcast.15, ...), custom_call_target="tpu_custom_call" | custom-call | tf_op jit(solution)/shard_map/pallas_call | solution.py:158
  51.5 0.0 copy-start.5
  51.6 0.0 copy-start.4
  51.6 0.0 copy-start.2
  51.6 0.0 copy-start.3
  51.6 0.7 copy-done.5
  52.3 0.1 copy-done.4
  52.3 0.0 copy-done.2
  52.3 0.0 copy-done.3
  52.4 69.3 %all-reduce.2 = (bf16[32,512]{1,0:T(8,128)(2,1)}, bf16[32,512]{1,0:T(8,128)(2,1)}, bf16[32,512]{1,0:T(8,128)(2,1)}, bf16[32,512]{1,0:T(8,128)(2,1)}, bf16[32,512...) all-reduce(bf16[32,512]{1,0:T(8,128)(2,1)S(1)} %copy-done.2, ...), channel_id=1, replica_groups=mesh['node'=64,'local'=16] {'local'}, use_global_device_ids=true, to_apply=%region_0.0 | all-reduce | flops 1048576 | bytes 4194304 | tf_op jit(solution)/shard_map/psum | solution.py:206
  121.6 6.9 %shard_map.87 = bf16[512,1024]{1,0:T(8,128)(2,1)} custom-call(bf16[32,512]{1,0:T(8,128)(2,1)} %get-tuple-element.138.refs_0_, bf16[32,512]{1,0:T(8,128)(2,1)} %get-tuple-element.139.refs_1_, bf16[32,512]{1,0:T(8,128)(2,1)} %get-tuple-element.140.refs_2_, bf16[32,512]{1,0:T(8,128)(2,1)} %get-tuple-element.141.refs_3_, ...), custom_call_target="tpu_custom_call" | custom-call | tf_op jit(solution)/shard_map/pallas_call | solution.py:158
  128.5 0.0 copy-start.6
  128.5 19.5 %all-to-all-start.1 = ((bf16[64,8,1024]{2,1,0:T(8,128)(2,1)}), bf16[64,8,1024]{2,1,0:T(8,128)(2,1)S(1)}, u32[]{:S(2)}, u32[]{:S(2)}) async-start(bf16[64,8,1024]{2,1,0:T(8,128)(2,1)} %bitcast.10), calls=%async_computation.1 | async-start | bytes 2097152 | tf_op jit(solution)/shard_map/all_to_all | solution.py:181
  148.1 0.0 copy-done.6
  148.1 0.1 copy.11.gates_ref
  148.1 27.9 %all-to-all-done.1 = bf16[64,8,1024]{2,1,0:T(8,128)(2,1)S(1)} async-done(((bf16[64,8,1024]{2,1,0:T(8,128)(2,1)}), bf16[64,8,1024]{2,1,0:T(8,128)(2,1)S(1)}, u32[]{:S(2)}, u32[]{:S(2)}) %all-to-all-start.1) | async-done | bytes 1048608 | tf_op jit(solution)/shard_map/all_to_all | solution.py:181
  176.0 1.3 shard_map.88
  177.4 0.7 copy.12
  (1 shorter events, 0.0 us)
Async XLA Ops:
  1.4 0.8 copy-start
  2.2 0.8 copy-start.1
  51.5 0.7 copy-start.5
  51.6 0.8 copy-start.4
  51.6 0.8 copy-start.2
  51.6 0.8 copy-start.3
  128.5 19.6 %copy-start.6 = (f32[32,8]{0,1:T(8,128)S(1)}, f32[32,8]{0,1:T(8,128)}, u32[]{:S(2)}) copy-start(f32[32,8]{0,1:T(8,128)} %param.9) | copy-start | bytes 3076
  128.5 47.5 %all-to-all-start.1 = ((bf16[64,8,1024]{2,1,0:T(8,128)(2,1)}), bf16[64,8,1024]{2,1,0:T(8,128)(2,1)S(1)}, u32[]{:S(2)}, u32[]{:S(2)}) async-start(bf16[64,8,1024]{2,1,0:T(8,128)(2,1)} %bitcast.10), calls=%async_computation.1 | async-start | bytes 2097152 | tf_op jit(solution)/shard_map/all_to_all | solution.py:181
where the time goes:
time: 179 us; the launch traced here: 178 us
  blocking collectives  113 us (63%)
  waiting for transfers between devices  27.9 us (16%)
  starting transfers between devices  19.5 us (11%)
  Pallas kernels  13.3 us (7%)
  local copies, waits for them, and re-layouts  3.8 us (2%)
    psum x1, blocking collectives, body(): sums = lax.psum(tuple(terms), 'local')  69.3 us
    all_to_all x1, blocking collectives, exchange(): lax.all_to_all(values.reshape(nodes, capacity, values.shape[1]), 'node',...  43.5 us
    all_to_all x1, waiting for transfers between devices, exchange(): lax.all_to_all(values.reshape(nodes, capacity, values.shape[1]), 'node',...  27.9 us
    all_to_all x1, starting transfers between devices, exchange(): lax.all_to_all(values.reshape(nodes, capacity, values.shape[1]), 'node',...  19.5 us
    pallas_call x4, Pallas kernels, call(): pl.pallas_call(kernel, out_shape=out_shape, in_specs=in_specs, out_specs=...  13.3 us
  transfers between devices with their start and end apart: 1, of which 1 were waited for; matrix products, arithmetic and copies ran while one was open for 0% of the time, Pallas kernels for 0%

commit v1 on v0

--- a/solution.py
+++ b/solution.py
@@ -11,8 +11,6 @@
 F32 = jnp.float32
 VMEM = pl.BlockSpec(memory_space=pltpu.VMEM)
 HBM = pl.BlockSpec(memory_space=pltpu.HBM)
-LARGE = 60 * 1024 * 1024
-SMALL = 16 * 1024 * 1024
 
 
 def pieces(rows, cols):
@@ -48,44 +46,54 @@
     return col // capacity, in_slot
 
 
-def pack_kernel(node_count, capacity, routes_ref, tokens_ref, cot_ref, sent_ref):
-    routes = routes_ref[...]
+def pack_kernel(node_count, capacity, routes_ref, tokens_ref, cot_ref, sent_ref, tokens_buf, cot_buf, sems):
+    copies = [
+        pltpu.make_async_copy(tokens_ref, tokens_buf, sems.at[0]),
+        pltpu.make_async_copy(cot_ref, cot_buf, sems.at[1]),
+    ]
+    for copy in copies:
+        copy.start()
+    routes = routes_ref[...].T
     expert, in_slot = slot_columns(routes, node_count, capacity)
     chosen = jnp.zeros(expert.shape, F32)
     for k in range(routes.shape[1]):
         chosen += jnp.where((routes[:, k : k + 1] == expert) & in_slot, 1.0, 0.0)
     chosen = chosen.T.astype(BF16)
-    both = jnp.concatenate([tokens_ref[...].astype(F32), cot_ref[...].astype(F32)], axis=1).astype(BF16)
+    for copy in copies:
+        copy.wait()
+    both = jnp.concatenate([tokens_buf[...].astype(F32), cot_buf[...].astype(F32)], axis=1).astype(BF16)
     sent_ref[...] = jnp.dot(chosen, both, preferred_element_type=F32).astype(BF16)
 
 
-def terms_kernel(parts, x_ref, w_in_ref, w_out_ref, *refs):
-    count = len(parts)
-    outs, (pre_ref, dact_ref, sems) = refs[: 2 * count], refs[2 * count :]
+def terms_kernel(parts, x_ref, w_in_hbm, w_out_hbm, *refs):
+    outs, (w_in_ref, w_out_ref, sems) = refs[: 2 * len(parts)], refs[2 * len(parts) :]
+    weights = [
+        pltpu.make_async_copy(w_in_hbm, w_in_ref, sems.at[0]),
+        pltpu.make_async_copy(w_out_hbm, w_out_ref, sems.at[1]),
+    ]
+    for copy in weights:
+        copy.start()
     feat = w_in_ref.shape[0]
     rows = x_ref.shape[0]
     step = min(128, rows)
-    copies = []
     for r0 in range(0, rows, step):
         band = slice(r0, r0 + step)
-        pre_ref[band] = jnp.dot(x_ref[band, :feat], w_in_ref[...], preferred_element_type=F32).astype(BF16)
-        dact_ref[band] = jnp.dot(x_ref[band, feat:], w_out_ref[...], preferred_element_type=F32).astype(BF16)
-        for first, source in ((0, pre_ref), (count, dact_ref)):
-            for i, (r, nr, c, nc) in enumerate(parts):
+        if r0 == 0:
+            weights[0].wait()
+        pre = jnp.dot(x_ref[band, :feat], w_in_ref[...], preferred_element_type=F32).astype(BF16)
+        if r0 == 0:
+            weights[1].wait()
+        dact = jnp.dot(x_ref[band, feat:], w_out_ref[...], preferred_element_type=F32).astype(BF16)
+        for value, refs in ((pre, outs[: len(parts)]), (dact, outs[len(parts) :])):
+            for (r, nr, c, nc), ref in zip(parts, refs):
                 if r0 <= r < r0 + step:
-                    copy = pltpu.make_async_copy(
-                        source.at[pl.ds(r, nr), pl.ds(c, nc)], outs[first + i], sems.at[first + i]
-                    )
-                    copy.start()
-                    copies.append(copy)
-    for copy in copies:
-        copy.wait()
+                    ref[...] = value[r - r0 : r - r0 + nr, c : c + nc]
 
 
 def outputs_kernel(parts, *refs):
     count = len(parts)
     sums = refs[: 2 * count]
-    w_in_ref, w_out_ref, back_ref, pre_ref, dact_ref, sems = refs[2 * count :]
+    w_in_hbm, w_out_hbm, back_ref, pre_ref, dact_ref, w_in_ref, w_out_ref, sems = refs[2 * count :]
     feat = w_in_ref.shape[0]
     rows, width = back_ref.shape
     half = width // 2
@@ -96,6 +104,12 @@
             copy = pltpu.make_async_copy(sums[first + i], target.at[pl.ds(r, nr), pl.ds(c, nc)], sems.at[first + i])
             copy.start()
             copies.append((r, copy))
+    weights = [
+        pltpu.make_async_copy(w_in_hbm, w_in_ref, sems.at[2 * count]),
+        pltpu.make_async_copy(w_out_hbm, w_out_ref, sems.at[2 * count + 1]),
+    ]
+    for copy in weights:
+        copy.start()
 
     for r0 in range(0, rows, step):
         for r, copy in copies:
@@ -111,6 +125,9 @@
         hi = inner.astype(BF16).astype(F32)
         mid = (inner - hi).astype(BF16).astype(F32)
         lo = inner - hi - mid
+        if r0 == 0:
+            for copy in weights:
+                copy.wait()
         y = lax.dot_general(act, w_out_ref[...], (((1,), (1,)), ((), ())), preferred_element_type=F32)
         dout = lax.dot_general(dpre, w_in_ref[...], (((1,), (1,)), ((), ())), preferred_element_type=F32)
         lane = lax.broadcasted_iota(jnp.int32, (step, half - feat), 1)
@@ -122,8 +139,8 @@
 
 
 def unpack_kernel(node_count, capacity, routes_ref, gates_ref, back_ref, mixed_ref, d_tokens_ref, d_gates_ref):
-    routes = routes_ref[...]
-    gates = gates_ref[...]
+    routes = routes_ref[...].T
+    gates = gates_ref[...].T
     tok, top = routes.shape
     feat = mixed_ref.shape[1]
     half = back_ref.shape[1] // 2
@@ -151,18 +168,22 @@
         got = jnp.dot(picks[k], back_ref[:, tail:half], preferred_element_type=F32)
         value = jnp.sum(jnp.where(lane >= feat - tail, got, 0.0), axis=1, keepdims=True)
         d_gates = jnp.where(column == k, value, d_gates)
-    d_gates_ref[...] = d_gates
-
-
-def call(kernel, in_specs, out_shape, out_space, *args, scratch=(), limit=SMALL):
+    d_gates_ref[...] = d_gates.T
+
+
+def call(kernel, in_specs, out_shape, *args, scratch=(), limit=16):
     return pl.pallas_call(
         kernel,
         out_shape=out_shape,
         in_specs=in_specs,
-        out_specs=jax.tree.map(lambda _: out_space, out_shape),
+        out_specs=jax.tree.map(lambda _: VMEM, out_shape),
         scratch_shapes=scratch,
-        compiler_params=pltpu.CompilerParams(vmem_limit_bytes=limit),
+        compiler_params=pltpu.CompilerParams(vmem_limit_bytes=limit * 1024 * 1024),
     )(*args)
+
+
+def in_hbm(*arrays):
+    return [pltpu.with_memory_space_constraint(array, pltpu.HBM) for array in arrays]
 
 
 def body(tokens, cotangent, routes, gate_probs, w_in, w_out):
@@ -175,7 +196,7 @@
     width = 2 * (-(-(feat + 3) // 128) * 128)
     parts = pieces(rows, hidden)
     up, down = w_in[0], w_out[0].T
-    scratch = [pltpu.VMEM((rows, hidden), BF16)] * 2 + [pltpu.SemaphoreType.DMA((2 * len(parts),))]
+    routes_t = routes.T
 
     def exchange(values):
         return lax.all_to_all(
@@ -184,51 +205,46 @@
 
     sent = call(
         functools.partial(pack_kernel, nodes, capacity),
-        [VMEM] * 3,
+        [VMEM, HBM, HBM],
         jax.ShapeDtypeStruct((rows, 2 * feat), BF16),
-        VMEM,
-        routes,
-        tokens,
-        cotangent,
+        routes_t,
+        *in_hbm(tokens, cotangent),
+        scratch=[pltpu.VMEM((tok, feat), BF16)] * 2 + [pltpu.SemaphoreType.DMA((2,))],
     )
     x_dy = exchange(sent)
     terms = call(
         functools.partial(terms_kernel, parts),
-        [VMEM] * 3,
-        tuple(jax.ShapeDtypeStruct((nr, nc), BF16) for _, nr, _, nc in parts) * 2,
-        HBM,
+        [VMEM, HBM, HBM],
+        tuple(pltpu.VMEM((nr, nc), BF16) for _, nr, _, nc in parts) * 2,
         x_dy,
-        up,
-        down,
-        scratch=scratch,
-        limit=LARGE,
+        *in_hbm(up, down),
+        scratch=[pltpu.VMEM((feat, hidden), BF16)] * 2 + [pltpu.SemaphoreType.DMA((2,))],
     )
     sums = lax.psum(tuple(terms), "local")
     back = call(
         functools.partial(outputs_kernel, parts),
-        [HBM] * len(sums) + [VMEM] * 2,
+        [HBM] * (len(sums) + 2),
         jax.ShapeDtypeStruct((rows, width), BF16),
-        VMEM,
-        *sums,
-        up,
-        down,
-        scratch=scratch,
-        limit=LARGE,
+        *in_hbm(*sums, up, down),
+        scratch=[pltpu.VMEM((rows, hidden), BF16)] * 2
+        + [pltpu.VMEM((feat, hidden), BF16)] * 2
+        + [pltpu.SemaphoreType.DMA((len(sums) + 2,))],
+        limit=32,
     )
     returned = exchange(back)
-    return call(
+    mixed, d_tokens, d_gates = call(
         functools.partial(unpack_kernel, nodes, capacity),
         [VMEM] * 3,
         (
             jax.ShapeDtypeStruct((tok, feat), BF16),
             jax.ShapeDtypeStruct((tok, feat), BF16),
-            jax.ShapeDtypeStruct((tok, top), F32),
+            jax.ShapeDtypeStruct((top, tok), F32),
         ),
-        VMEM,
-        routes,
-        gate_probs,
+        routes_t,
+        gate_probs.T,
         returned,
     )
+    return mixed, d_tokens, d_gates.T
 
 
 def solution(mesh):

time: 179 us -> 173 us (0.966)
  blocking collectives: 113 us -> 160 us
  waiting for transfers between devices: 27.9 us -> 0 us
  starting transfers between devices: 19.5 us -> 0 us
  local copies, waits for them, and re-layouts: 3.8 us -> 0.69 us
  Pallas kernels: 13.3 us -> 11.2 us
    all_to_all x1 -> x2, blocking collectives: 43.5 us -> 90 us  [exchange(): lax.all_to_all(values.reshape(nodes, capacity, values.shape[1]), 'node',...]
    all_to_all x1 -> x0, waiting for transfers between devices: 27.9 us -> none  [exchange(): lax.all_to_all(values.reshape(nodes, capacity, values.shape[1]), 'node',...]
    all_to_all x1 -> x0, starting transfers between devices: 19.5 us -> none  [exchange(): lax.all_to_all(values.reshape(nodes, capacity, values.shape[1]), 'node',...]
    unnamed x16 -> x6, local copies, waits for them, and re-layouts: 3.14 us -> 0.69 us
    pallas_call x4, Pallas kernels: 13.3 us -> 11.2 us  [call(): pl.pallas_call(kernel, out_shape=out_shape, in_specs=in_specs, out_specs=...]
  transfers between devices with their start and end apart: 1 -> 0, of which waited for: 1 -> 0; matrix products, arithmetic and copies ran while one was open for 0% -> 0% of each run, Pallas kernels for 0% -> 0%
where the time goes in v1:
time: 173 us
  blocking collectives  160 us (92%)
  Pallas kernels  11.2 us (6%)
    all_to_all x2, blocking collectives, exchange(): lax.all_to_all(values.reshape(nodes, capacity, values.shape[1]), 'node',...  90 us
    psum x1, blocking collectives, body(): sums = lax.psum(tuple(terms), 'local')  70.4 us
    pallas_call x4, Pallas kernels, call(): pl.pallas_call(kernel, out_shape=out_shape, in_specs=in_specs, out_specs=...  11.2 us

profile of v1, /device:TPU:1, one launch (start us, length us, event | category | flops | bytes accessed | tf_op | source)
XLA Modules:
  0.0 172.9 jit_solution(2833228150465227107)
XLA Ops:
  0.6 0.0 copy-start
  0.6 0.7 copy-done
  1.3 1.2 shard_map.85
  2.5 42.8 %all_to_all.10 = bf16[64,8,896]{2,1,0:T(8,128)(2,1)S(1)} all-to-all(bf16[64,8,896]{2,1,0:T(8,128)(2,1)S(1)} %bitcast.13), channel_id=1, replica_groups=mesh['node'=64,'local'=16] {'node'}, dimensions={0} | all-to-all | bytes 1835008 | tf_op jit(solution)/shard_map/all_to_all | solution.py:202
  45.3 2.7 %shard_map.86 = (bf16[32,512]{1,0:T(8,128)(2,1)S(1)}, bf16[32,512]{1,0:T(8,128)(2,1)S(1)}, bf16[32,512]{1,0:T(8,128)(2,1)S(1)}, bf16[32,512]{1,0:T(8,128)(2,1)S(...) custom-call(bf16[512,896]{1,0:T(8,128)(2,1)S(1)} %bitcast.14, ...), custom_call_target="tpu_custom_call" | custom-call | tf_op jit(solution)/shard_map/pallas_call | solution.py:175
  48.0 70.4 %all-reduce.2 = (bf16[32,512]{1,0:T(8,128)(2,1)}, bf16[32,512]{1,0:T(8,128)(2,1)}, bf16[32,512]{1,0:T(8,128)(2,1)}, bf16[32,512]{1,0:T(8,128)(2,1)}, bf16[32,512...) all-reduce(bf16[32,512]{1,0:T(8,128)(2,1)S(1)} %get-tuple-element.7, ...), channel_id=1, replica_groups=mesh['node'=64,'local'=16] {'local'}, use_global_device_ids=true, to_apply=%region_0.0 | all-reduce | flops 1048576 | bytes 4194304 | tf_op jit(solution)/shard_map/psum | solution.py:223
  118.4 5.7 %shard_map.87 = bf16[512,1024]{1,0:T(8,128)(2,1)S(1)} custom-call(bf16[32,512]{1,0:T(8,128)(2,1)} %get-tuple-element.141.refs_0_, bf16[32,512]{1,0:T(8,128)(2,1)} %get-tuple-element.142.refs_1_, bf16[32,512]{1,0:T(8,128)(2,1)} %get-tuple-element.143.refs_2_, bf16[32,512]{1,0:T(8,128)(2,1)} %get-tuple-element.144.refs_3_, ...), custom_call_target="tpu_custom_call" | custom-call | tf_op jit(solution)/shard_map/pallas_call | solution.py:175
  124.1 0.0 copy-start.1
  124.1 0.0 copy-start.2
  124.1 47.2 %all_to_all.11 = bf16[64,8,1024]{2,1,0:T(8,128)(2,1)S(1)} all-to-all(bf16[64,8,1024]{2,1,0:T(8,128)(2,1)S(1)} %bitcast.11), channel_id=1, replica_groups=mesh['node'=64,'local'=16] {'node'}, dimensions={0} | all-to-all | bytes 2097152 | tf_op jit(solution)/shard_map/all_to_all | solution.py:202
  171.3 0.0 copy-done.1
  171.3 0.0 copy-done.2
  171.3 1.7 shard_map.88
Async XLA Ops:
  0.6 0.7 copy-start
  124.1 47.2 %copy-start.1 = (s32[32,8]{0,1:T(8,128)S(1)}, s32[32,8]{0,1:T(8,128)}, u32[]{:S(2)}) copy-start(s32[32,8]{0,1:T(8,128)} %param.8) | copy-start | bytes 3076
  124.1 47.2 %copy-start.2 = (f32[32,8]{0,1:T(8,128)S(1)}, f32[32,8]{0,1:T(8,128)}, u32[]{:S(2)}) copy-start(f32[32,8]{0,1:T(8,128)} %param.9) | copy-start | bytes 3076

commit v2 on v1

--- a/solution.py
+++ b/solution.py
@@ -14,15 +14,9 @@
 
 
 def pieces(rows, cols):
-    half = cols // 2
-    out = []
-    for r in range(0, rows, 32):
-        out.append((r, 32, 0, half))
-        out.append((r, 32, half, half))
-    r, nr, c, nc = out.pop()
-    out.append((r, nr, c, nc // 2))
-    out.append((r, nr, c + nc // 2, nc // 2))
-    return out
+    out = [(r, 16, 0, cols) for r in range(0, rows, 16)]
+    r, nr, _, _ = out.pop()
+    return out + [(r, nr, 0, cols // 2), (r, nr, cols // 2, cols // 2)]
 
 
 def slot_columns(routes, node_count, capacity):
@@ -46,20 +40,22 @@
     return col // capacity, in_slot
 
 
-def pack_kernel(node_count, capacity, routes_ref, tokens_ref, cot_ref, sent_ref, tokens_buf, cot_buf, sems):
+def pack_kernel(node_count, capacity, routes_ref, tokens_ref, cot_ref, sent_ref, tokens_buf, cot_buf, routes_buf, sems):
     copies = [
         pltpu.make_async_copy(tokens_ref, tokens_buf, sems.at[0]),
         pltpu.make_async_copy(cot_ref, cot_buf, sems.at[1]),
-    ]
-    for copy in copies:
+        pltpu.make_async_copy(routes_ref, routes_buf, sems.at[2]),
+    ]
+    for copy in copies[::-1]:
         copy.start()
-    routes = routes_ref[...].T
+    copies[2].wait()
+    routes = routes_buf[...].T
     expert, in_slot = slot_columns(routes, node_count, capacity)
     chosen = jnp.zeros(expert.shape, F32)
     for k in range(routes.shape[1]):
         chosen += jnp.where((routes[:, k : k + 1] == expert) & in_slot, 1.0, 0.0)
     chosen = chosen.T.astype(BF16)
-    for copy in copies:
+    for copy in copies[:2]:
         copy.wait()
     both = jnp.concatenate([tokens_buf[...].astype(F32), cot_buf[...].astype(F32)], axis=1).astype(BF16)
     sent_ref[...] = jnp.dot(chosen, both, preferred_element_type=F32).astype(BF16)
@@ -98,17 +94,16 @@
     rows, width = back_ref.shape
     half = width // 2
     step = min(128, rows)
-    copies = []
-    for i, (r, nr, c, nc) in enumerate(parts):
-        for first, target in ((0, pre_ref), (count, dact_ref)):
-            copy = pltpu.make_async_copy(sums[first + i], target.at[pl.ds(r, nr), pl.ds(c, nc)], sems.at[first + i])
-            copy.start()
-            copies.append((r, copy))
+    copies = [
+        (r, pltpu.make_async_copy(sums[first + i], target.at[pl.ds(r, nr), pl.ds(c, nc)], sems.at[first + i]))
+        for i, (r, nr, c, nc) in enumerate(parts)
+        for first, target in ((0, pre_ref), (count, dact_ref))
+    ]
     weights = [
-        pltpu.make_async_copy(w_in_hbm, w_in_ref, sems.at[2 * count]),
-        pltpu.make_async_copy(w_out_hbm, w_out_ref, sems.at[2 * count + 1]),
-    ]
-    for copy in weights:
+        pltpu.make_async_copy(w_out_hbm, w_out_ref, sems.at[2 * count]),
+        pltpu.make_async_copy(w_in_hbm, w_in_ref, sems.at[2 * count + 1]),
+    ]
+    for copy in [copy for r, copy in copies if r < step] + weights + [copy for r, copy in copies if r >= step]:
         copy.start()
 
     for r0 in range(0, rows, step):
@@ -118,9 +113,10 @@
         band = slice(r0, r0 + step)
         pre = pre_ref[band].astype(F32)
         dact = dact_ref[band].astype(F32)
-        sig = 1.0 / (1.0 + jnp.exp(-pre))
-        act = (pre * sig).astype(BF16)
-        dpre = (dact * sig * (1.0 + pre * (1.0 - sig))).astype(BF16)
+        sig = 0.5 * jnp.tanh(0.5 * pre) + 0.5
+        silu = pre * sig
+        act = silu.astype(BF16)
+        dpre = (dact * (sig + silu * (1.0 - sig))).astype(BF16)
         inner = jnp.sum(act.astype(F32) * dact, axis=1, keepdims=True)
         hi = inner.astype(BF16).astype(F32)
         mid = (inner - hi).astype(BF16).astype(F32)
@@ -205,11 +201,11 @@
 
     sent = call(
         functools.partial(pack_kernel, nodes, capacity),
-        [VMEM, HBM, HBM],
+        [HBM] * 3,
         jax.ShapeDtypeStruct((rows, 2 * feat), BF16),
-        routes_t,
-        *in_hbm(tokens, cotangent),
-        scratch=[pltpu.VMEM((tok, feat), BF16)] * 2 + [pltpu.SemaphoreType.DMA((2,))],
+        *in_hbm(routes_t, tokens, cotangent),
+        scratch=[pltpu.VMEM((tok, feat), BF16)] * 2
+        + [pltpu.VMEM((top, tok), jnp.int32), pltpu.SemaphoreType.DMA((3,))],
     )
     x_dy = exchange(sent)
     terms = call(

time: 173 us -> 173 us (level)
  no operation moved by 1% of the time
where the time goes in v2:
time: 173 us; the launch traced here: 172 us
  blocking collectives  160 us (92%)
  Pallas kernels  11.2 us (6%)
    all_to_all x2, blocking collectives, exchange(): lax.all_to_all(values.reshape(nodes, capacity, values.shape[1]), 'node',...  90.1 us
    psum x1, blocking collectives, body(): sums = lax.psum(tuple(terms), 'local')  70.3 us
    pallas_call x4, Pallas kernels, call(): pl.pallas_call(kernel, out_shape=out_shape, in_specs=in_specs, out_specs=...  11.2 us

profile of v2, /device:TPU:1, one launch (start us, length us, event | category | flops | bytes accessed | tf_op | source)
XLA Modules:
  0.0 172.3 jit_solution(2785504776448524196)
XLA Ops:
  0.6 1.7 shard_map.85
  2.3 42.8 %all_to_all.10 = bf16[64,8,896]{2,1,0:T(8,128)(2,1)S(1)} all-to-all(bf16[64,8,896]{2,1,0:T(8,128)(2,1)S(1)} %bitcast.13), channel_id=1, replica_groups=mesh['node'=64,'local'=16] {'node'}, dimensions={0} | all-to-all | bytes 1835008 | tf_op jit(solution)/shard_map/all_to_all | solution.py:198
  45.2 2.7 %shard_map.86 = (bf16[16,1024]{1,0:T(8,128)(2,1)S(1)}, bf16[16,1024]{1,0:T(8,128)(2,1)S(1)}, bf16[16,1024]{1,0:T(8,128)(2,1)S(1)}, bf16[16,1024]{1,0:T(8,128)(2,...) custom-call(bf16[512,896]{1,0:T(8,128)(2,1)S(1)} %bitcast.14, ...), custom_call_target="tpu_custom_call" | custom-call | tf_op jit(solution)/shard_map/pallas_call | solution.py:171
  47.8 70.3 %all-reduce.2 = (bf16[16,1024]{1,0:T(8,128)(2,1)}, bf16[16,1024]{1,0:T(8,128)(2,1)}, bf16[16,1024]{1,0:T(8,128)(2,1)}, bf16[16,1024]{1,0:T(8,128)(2,1)}, bf16[16...) all-reduce(bf16[16,1024]{1,0:T(8,128)(2,1)S(1)} %get-tuple-element., ...), channel_id=1, replica_groups=mesh['node'=64,'local'=16] {'local'}, use_global_device_ids=true, to_apply=%region_0.0 | all-reduce | flops 1048576 | bytes 4194304 | tf_op jit(solution)/shard_map/psum | solution.py:219
  118.1 5.2 %shard_map.87 = bf16[512,1024]{1,0:T(8,128)(2,1)S(1)} custom-call(bf16[16,1024]{1,0:T(8,128)(2,1)} %get-tuple-element.141.refs_0_, bf16[16,1024]{1,0:T(8,128)(2,1)} %get-tuple-element.142.refs_1_, bf16[16,1024]{1,0:T(8,128)(2,1)} %get-tuple-element.143.refs_2_, bf16[16,1024]{1,0:T(8,128)(2,1)} %get-tuple-element.144.refs_3_, ...), custom_call_target="tpu_custom_call" | custom-call | tf_op jit(solution)/shard_map/pallas_call | solution.py:171
  123.3 0.0 copy-start
  123.3 0.0 copy-start.1
  123.3 47.3 %all_to_all.11 = bf16[64,8,1024]{2,1,0:T(8,128)(2,1)S(1)} all-to-all(bf16[64,8,1024]{2,1,0:T(8,128)(2,1)S(1)} %bitcast.11), channel_id=1, replica_groups=mesh['node'=64,'local'=16] {'node'}, dimensions={0} | all-to-all | bytes 2097152 | tf_op jit(solution)/shard_map/all_to_all | solution.py:198
  170.6 0.0 copy-done
  170.6 0.0 copy-done.1
  170.6 1.7 shard_map.88
Async XLA Ops:
  123.3 47.3 %copy-start = (s32[32,8]{0,1:T(8,128)S(1)}, s32[32,8]{0,1:T(8,128)}, u32[]{:S(2)}) copy-start(s32[32,8]{0,1:T(8,128)} %param.8) | copy-start | bytes 3076
  123.3 47.3 %copy-start.1 = (f32[32,8]{0,1:T(8,128)S(1)}, f32[32,8]{0,1:T(8,128)}, u32[]{:S(2)}) copy-start(f32[32,8]{0,1:T(8,128)} %param.9) | copy-start | bytes 3076

commit v3 on v2

--- a/solution.py
+++ b/solution.py
@@ -72,16 +72,14 @@
     feat = w_in_ref.shape[0]
     rows = x_ref.shape[0]
     step = min(128, rows)
-    for r0 in range(0, rows, step):
-        band = slice(r0, r0 + step)
-        if r0 == 0:
-            weights[0].wait()
-        pre = jnp.dot(x_ref[band, :feat], w_in_ref[...], preferred_element_type=F32).astype(BF16)
-        if r0 == 0:
-            weights[1].wait()
-        dact = jnp.dot(x_ref[band, feat:], w_out_ref[...], preferred_element_type=F32).astype(BF16)
-        for value, refs in ((pre, outs[: len(parts)]), (dact, outs[len(parts) :])):
-            for (r, nr, c, nc), ref in zip(parts, refs):
+    sides = ((0, w_in_ref, outs[: len(parts)]), (feat, w_out_ref, outs[len(parts) :]))
+    for (first, weight_ref, side_outs), copy in zip(sides, weights):
+        copy.wait()
+        for r0 in range(0, rows, step):
+            value = jnp.dot(
+                x_ref[r0 : r0 + step, first : first + feat], weight_ref[...], preferred_element_type=F32
+            ).astype(BF16)
+            for (r, nr, c, nc), ref in zip(parts, side_outs):
                 if r0 <= r < r0 + step:
                     ref[...] = value[r - r0 : r - r0 + nr, c : c + nc]
 
@@ -93,7 +91,7 @@
     feat = w_in_ref.shape[0]
     rows, width = back_ref.shape
     half = width // 2
-    step = min(128, rows)
+    step = min(256, rows)
     copies = [
         (r, pltpu.make_async_copy(sums[first + i], target.at[pl.ds(r, nr), pl.ds(c, nc)], sems.at[first + i]))
         for i, (r, nr, c, nc) in enumerate(parts)
@@ -106,7 +104,7 @@
     for copy in [copy for r, copy in copies if r < step] + weights + [copy for r, copy in copies if r >= step]:
         copy.start()
 
-    for r0 in range(0, rows, step):
+    def activations(r0):
         for r, copy in copies:
             if r0 <= r < r0 + step:
                 copy.wait()
@@ -118,12 +116,19 @@
         act = silu.astype(BF16)
         dpre = (dact * (sig + silu * (1.0 - sig))).astype(BF16)
         inner = jnp.sum(act.astype(F32) * dact, axis=1, keepdims=True)
+        return act, dpre, inner
+
+    ready = activations(0)
+    for copy in weights:
+        copy.wait()
+    for r0 in range(0, rows, step):
+        act, dpre, inner = ready
+        if r0 + step < rows:
+            ready = activations(r0 + step)
+        band = slice(r0, r0 + step)
         hi = inner.astype(BF16).astype(F32)
         mid = (inner - hi).astype(BF16).astype(F32)
         lo = inner - hi - mid
-        if r0 == 0:
-            for copy in weights:
-                copy.wait()
         y = lax.dot_general(act, w_out_ref[...], (((1,), (1,)), ((), ())), preferred_element_type=F32)
         dout = lax.dot_general(dpre, w_in_ref[...], (((1,), (1,)), ((), ())), preferred_element_type=F32)
         lane = lax.broadcasted_iota(jnp.int32, (step, half - feat), 1)
@@ -134,36 +139,40 @@
         back_ref[band, half + feat :] = jnp.zeros((step, half - feat), BF16)
 
 
-def unpack_kernel(node_count, capacity, routes_ref, gates_ref, back_ref, mixed_ref, d_tokens_ref, d_gates_ref):
+def places_kernel(node_count, capacity, routes_ref, gates_ref, stack_ref):
     routes = routes_ref[...].T
     gates = gates_ref[...].T
     tok, top = routes.shape
-    feat = mixed_ref.shape[1]
-    half = back_ref.shape[1] // 2
     expert, in_slot = slot_columns(routes, node_count, capacity)
     weight = jnp.zeros(expert.shape, F32)
-    picks = []
     for k in range(top):
         mine = (routes[:, k : k + 1] == expert) & in_slot
         weight += jnp.where(mine, gates[:, k : k + 1], 0.0)
-        picks.append(jnp.where(mine, 1.0, 0.0).astype(BF16))
+        stack_ref[(3 + k) * tok : (4 + k) * tok] = jnp.where(mine, 1.0, 0.0).astype(BF16)
     hi = weight.astype(BF16)
     rest = weight - hi.astype(F32)
     mid = rest.astype(BF16)
-    lo = (rest - mid.astype(F32)).astype(BF16)
-    stack = jnp.concatenate([hi, mid, lo], axis=0)
-    out = jnp.dot(stack, back_ref[...], preferred_element_type=F32)
+    stack_ref[:tok] = hi
+    stack_ref[tok : 2 * tok] = mid
+    stack_ref[2 * tok : 3 * tok] = (rest - mid.astype(F32)).astype(BF16)
+
+
+def unpack_kernel(stack_ref, back_ref, mixed_ref, d_tokens_ref, d_gates_ref):
+    tok, feat = mixed_ref.shape
+    top = d_gates_ref.shape[0]
+    half = back_ref.shape[1] // 2
+    out = jnp.dot(stack_ref[: 3 * tok], back_ref[...], preferred_element_type=F32)
     out = out[:tok] + (out[tok : 2 * tok] + out[2 * tok :])
     mixed_ref[...] = out[:, :feat].astype(BF16)
     d_tokens_ref[...] = out[:, half : half + feat].astype(BF16)
     tail = half - 128
     lane = lax.broadcasted_iota(jnp.int32, (1, 128), 1)
     column = lax.broadcasted_iota(jnp.int32, (tok, top), 1)
+    got = jnp.dot(stack_ref[3 * tok :], back_ref[:, tail:half], preferred_element_type=F32)
+    values = jnp.sum(jnp.where(lane >= feat - tail, got, 0.0), axis=1, keepdims=True)
     d_gates = jnp.zeros((tok, top), F32)
     for k in range(top):
-        got = jnp.dot(picks[k], back_ref[:, tail:half], preferred_element_type=F32)
-        value = jnp.sum(jnp.where(lane >= feat - tail, got, 0.0), axis=1, keepdims=True)
-        d_gates = jnp.where(column == k, value, d_gates)
+        d_gates = jnp.where(column == k, values[k * tok : (k + 1) * tok], d_gates)
     d_gates_ref[...] = d_gates.T
 
 
@@ -227,17 +236,24 @@
         + [pltpu.SemaphoreType.DMA((len(sums) + 2,))],
         limit=32,
     )
+    late_routes, late_gates, back = lax.optimization_barrier((routes_t, gate_probs.T, back))
+    places = call(
+        functools.partial(places_kernel, nodes, capacity),
+        [VMEM] * 2,
+        jax.ShapeDtypeStruct(((3 + top) * tok, rows), BF16),
+        late_routes,
+        late_gates,
+    )
     returned = exchange(back)
     mixed, d_tokens, d_gates = call(
-        functools.partial(unpack_kernel, nodes, capacity),
-        [VMEM] * 3,
+        unpack_kernel,
+        [VMEM] * 2,
         (
             jax.ShapeDtypeStruct((tok, feat), BF16),
             jax.ShapeDtypeStruct((tok, feat), BF16),
             jax.ShapeDtypeStruct((top, tok), F32),
         ),
-        routes_t,
-        gate_probs.T,
+        places,
         returned,
     )
     return mixed, d_tokens, d_gates.T

time: 173 us -> 172 us (level)
  blocking collectives: 160 us -> 113 us
  waiting for transfers between devices: 0 us -> 27.4 us
  starting transfers between devices: 0 us -> 19.5 us
    all_to_all x2 -> x1, blocking collectives: 90.1 us -> 42.8 us  [exchange(): lax.all_to_all(values.reshape(nodes, capacity, values.shape[1]), 'node',...]
    all_to_all x0 -> x1, waiting for transfers between devices: none -> 27.4 us  [exchange(): lax.all_to_all(values.reshape(nodes, capacity, values.shape[1]), 'node',...]
    all_to_all x0 -> x1, starting transfers between devices: none -> 19.5 us  [exchange(): lax.all_to_all(values.reshape(nodes, capacity, values.shape[1]), 'node',...]
    pallas_call x4 -> x5, Pallas kernels: 11.2 us -> 10.9 us  [call(): pl.pallas_call(kernel, out_shape=out_shape, in_specs=in_specs, out_specs=...]
  transfers between devices with their start and end apart: 0 -> 1, of which waited for: 0 -> 1; matrix products, arithmetic and copies ran while one was open for 0% -> 0% of each run, Pallas kernels for 0% -> 0%
where the time goes in v3:
time: 172 us
  blocking collectives  113 us (66%)
  waiting for transfers between devices  27.4 us (16%)
  starting transfers between devices  19.5 us (11%)
  Pallas kernels  10.9 us (6%)
    psum x1, blocking collectives, body(): sums = lax.psum(tuple(terms), 'local')  70.3 us
    all_to_all x1, blocking collectives, exchange(): lax.all_to_all(values.reshape(nodes, capacity, values.shape[1]), 'node',...  42.8 us
    all_to_all x1, waiting for transfers between devices, exchange(): lax.all_to_all(values.reshape(nodes, capacity, values.shape[1]), 'node',...  27.4 us
    all_to_all x1, starting transfers between devices, exchange(): lax.all_to_all(values.reshape(nodes, capacity, values.shape[1]), 'node',...  19.5 us
    pallas_call x5, Pallas kernels, call(): pl.pallas_call(kernel, out_shape=out_shape, in_specs=in_specs, out_specs=...  10.9 us
  transfers between devices with their start and end apart: 1, of which 1 were waited for; matrix products, arithmetic and copies ran while one was open for 0% of the time, Pallas kernels for 0%

profile of v3, /device:TPU:1, one launch (start us, length us, event | category | flops | bytes accessed | tf_op | source)
XLA Modules:
  0.0 171.7 jit_solution(10940180297629621230)
XLA Ops:
  0.6 1.7 shard_map.85
  2.3 42.8 %all_to_all.10 = bf16[64,8,896]{2,1,0:T(8,128)(2,1)S(1)} all-to-all(bf16[64,8,896]{2,1,0:T(8,128)(2,1)S(1)} %bitcast.12), channel_id=1, replica_groups=mesh['node'=64,'local'=16] {'node'}, dimensions={0} | all-to-all | bytes 1835008 | tf_op jit(solution)/shard_map/all_to_all | solution.py:207
  45.2 2.7 %shard_map.86 = (bf16[16,1024]{1,0:T(8,128)(2,1)S(1)}, bf16[16,1024]{1,0:T(8,128)(2,1)S(1)}, bf16[16,1024]{1,0:T(8,128)(2,1)S(1)}, bf16[16,1024]{1,0:T(8,128)(2,...) custom-call(bf16[512,896]{1,0:T(8,128)(2,1)S(1)} %bitcast.13, ...), custom_call_target="tpu_custom_call" | custom-call | tf_op jit(solution)/shard_map/pallas_call | solution.py:180
  47.8 70.3 %all-reduce.2 = (bf16[16,1024]{1,0:T(8,128)(2,1)}, bf16[16,1024]{1,0:T(8,128)(2,1)}, bf16[16,1024]{1,0:T(8,128)(2,1)}, bf16[16,1024]{1,0:T(8,128)(2,1)}, bf16[16...) all-reduce(bf16[16,1024]{1,0:T(8,128)(2,1)S(1)} %get-tuple-element., ...), channel_id=1, replica_groups=mesh['node'=64,'local'=16] {'local'}, use_global_device_ids=true, to_apply=%region_0.0 | all-reduce | flops 1048576 | bytes 4194304 | tf_op jit(solution)/shard_map/psum | solution.py:228
  118.1 4.9 %shard_map.87 = bf16[512,1024]{1,0:T(8,128)(2,1)} custom-call(bf16[16,1024]{1,0:T(8,128)(2,1)} %get-tuple-element.147.refs_0_, bf16[16,1024]{1,0:T(8,128)(2,1)} %get-tuple-element.148.refs_1_, bf16[16,1024]{1,0:T(8,128)(2,1)} %get-tuple-element.149.refs_2_, bf16[16,1024]{1,0:T(8,128)(2,1)} %get-tuple-element.150.refs_3_, ...), custom_call_target="tpu_custom_call" | custom-call | tf_op jit(solution)/shard_map/pallas_call | solution.py:180
  123.0 0.0 copy-start
  123.0 0.0 copy-start.1
  123.0 19.5 %all-to-all-start.1 = ((bf16[64,8,1024]{2,1,0:T(8,128)(2,1)}), bf16[64,8,1024]{2,1,0:T(8,128)(2,1)S(1)}, u32[]{:S(2)}, u32[]{:S(2)}) async-start(bf16[64,8,1024]{2,1,0:T(8,128)(2,1)} %bitcast.7), calls=%async_computation.1 | async-start | bytes 2097152 | tf_op jit(solution)/shard_map/all_to_all | solution.py:207
  142.6 0.0 copy-done
  142.6 0.0 copy-done.1
  142.6 0.5 shard_map.88.stack_ref
  143.1 27.4 %all-to-all-done.1 = bf16[64,8,1024]{2,1,0:T(8,128)(2,1)S(1)} async-done(((bf16[64,8,1024]{2,1,0:T(8,128)(2,1)}), bf16[64,8,1024]{2,1,0:T(8,128)(2,1)S(1)}, u32[]{:S(2)}, u32[]{:S(2)}) %all-to-all-start.1) | async-done | bytes 1048608 | tf_op jit(solution)/shard_map/all_to_all | solution.py:207
  170.6 1.1 shard_map.89
Async XLA Ops:
  123.0 19.6 %copy-start = (s32[32,8]{0,1:T(8,128)S(1)}, s32[32,8]{0,1:T(8,128)}, u32[]{:S(2)}) copy-start(s32[32,8]{0,1:T(8,128)} %param.8) | copy-start | bytes 3076
  123.0 19.6 %copy-start.1 = (f32[32,8]{0,1:T(8,128)S(1)}, f32[32,8]{0,1:T(8,128)}, u32[]{:S(2)}) copy-start(f32[32,8]{0,1:T(8,128)} %param.9) | copy-start | bytes 3076
  123.0 47.5 %all-to-all-start.1 = ((bf16[64,8,1024]{2,1,0:T(8,128)(2,1)}), bf16[64,8,1024]{2,1,0:T(8,128)(2,1)S(1)}, u32[]{:S(2)}, u32[]{:S(2)}) async-start(bf16[64,8,1024]{2,1,0:T(8,128)(2,1)} %bitcast.7), calls=%async_computation.1 | async-start | bytes 2097152 | tf_op jit(solution)/shard_map/all_to_all | solution.py:207

commit v4 on v3

--- a/solution.py
+++ b/solution.py
@@ -84,7 +84,7 @@
                     ref[...] = value[r - r0 : r - r0 + nr, c : c + nc]
 
 
-def outputs_kernel(parts, *refs):
+def outputs_kernel(parts, near, *refs):
     count = len(parts)
     sums = refs[: 2 * count]
     w_in_hbm, w_out_hbm, back_ref, pre_ref, dact_ref, w_in_ref, w_out_ref, sems = refs[2 * count :]
@@ -96,6 +96,7 @@
         (r, pltpu.make_async_copy(sums[first + i], target.at[pl.ds(r, nr), pl.ds(c, nc)], sems.at[first + i]))
         for i, (r, nr, c, nc) in enumerate(parts)
         for first, target in ((0, pre_ref), (count, dact_ref))
+        if i >= near
     ]
     weights = [
         pltpu.make_async_copy(w_out_hbm, w_out_ref, sems.at[2 * count]),
@@ -103,14 +104,20 @@
     ]
     for copy in [copy for r, copy in copies if r < step] + weights + [copy for r, copy in copies if r >= step]:
         copy.start()
+
+    def band_of(r0, first, held):
+        values = [sums[first + i][...] for i, (r, _, _, _) in enumerate(parts[:near]) if r0 <= r < r0 + step]
+        done = r0 + sum(value.shape[0] for value in values)
+        if done < r0 + step:
+            values.append(held[done : r0 + step])
+        return jnp.concatenate(values, axis=0).astype(F32)
 
     def activations(r0):
         for r, copy in copies:
             if r0 <= r < r0 + step:
                 copy.wait()
-        band = slice(r0, r0 + step)
-        pre = pre_ref[band].astype(F32)
-        dact = dact_ref[band].astype(F32)
+        pre = band_of(r0, 0, pre_ref)
+        dact = band_of(r0, count, dact_ref)
         sig = 0.5 * jnp.tanh(0.5 * pre) + 0.5
         silu = pre * sig
         act = silu.astype(BF16)
@@ -226,11 +233,15 @@
         scratch=[pltpu.VMEM((feat, hidden), BF16)] * 2 + [pltpu.SemaphoreType.DMA((2,))],
     )
     sums = lax.psum(tuple(terms), "local")
+    near = (len(parts) - 1) // 2
+    spaces = [VMEM if i % len(parts) < near else HBM for i in range(len(sums))]
+    placed = [pltpu.with_memory_space_constraint(part, spec.memory_space) for part, spec in zip(sums, spaces)]
     back = call(
-        functools.partial(outputs_kernel, parts),
-        [HBM] * (len(sums) + 2),
+        functools.partial(outputs_kernel, parts, near),
+        spaces + [HBM] * 2,
         jax.ShapeDtypeStruct((rows, width), BF16),
-        *in_hbm(*sums, up, down),
+        *placed,
+        *in_hbm(up, down),
         scratch=[pltpu.VMEM((rows, hidden), BF16)] * 2
         + [pltpu.VMEM((feat, hidden), BF16)] * 2
         + [pltpu.SemaphoreType.DMA((len(sums) + 2,))],

time: 172 us -> 172 us (level)
  no operation moved by 1% of the time
where the time goes in v4:
time: 172 us; the launch traced here: 171 us
  blocking collectives  113 us (66%)
  waiting for transfers between devices  27.4 us (16%)
  starting transfers between devices  19.5 us (11%)
  Pallas kernels  10.6 us (6%)
    psum x1, blocking collectives, body(): sums = lax.psum(tuple(terms), 'local')  70.4 us
    all_to_all x1, blocking collectives, exchange(): lax.all_to_all(values.reshape(nodes, capacity, values.shape[1]), 'node',...  42.8 us
    all_to_all x1, waiting for transfers between devices, exchange(): lax.all_to_all(values.reshape(nodes, capacity, values.shape[1]), 'node',...  27.4 us
    all_to_all x1, starting transfers between devices, exchange(): lax.all_to_all(values.reshape(nodes, capacity, values.shape[1]), 'node',...  19.5 us
    pallas_call x5, Pallas kernels, call(): pl.pallas_call(kernel, out_shape=out_shape, in_specs=in_specs, out_specs=...  10.6 us
  transfers between devices with their start and end apart: 1, of which 1 were waited for; matrix products, arithmetic and copies ran while one was open for 0% of the time, Pallas kernels for 0%

profile of v4, /device:TPU:1, one launch (start us, length us, event | category | flops | bytes accessed | tf_op | source)
XLA Modules:
  0.0 171.5 jit_solution(9723923545628093392)
XLA Ops:
  0.6 1.7 shard_map.85
  2.3 42.8 %all_to_all.10 = bf16[64,8,896]{2,1,0:T(8,128)(2,1)S(1)} all-to-all(bf16[64,8,896]{2,1,0:T(8,128)(2,1)S(1)} %bitcast.12), channel_id=1, replica_groups=mesh['node'=64,'local'=16] {'node'}, dimensions={0} | all-to-all | bytes 1835008 | tf_op jit(solution)/shard_map/all_to_all | solution.py:214
  45.2 2.7 %shard_map.86 = (bf16[16,1024]{1,0:T(8,128)(2,1)S(1)}, bf16[16,1024]{1,0:T(8,128)(2,1)S(1)}, bf16[16,1024]{1,0:T(8,128)(2,1)S(1)}, bf16[16,1024]{1,0:T(8,128)(2,...) custom-call(bf16[512,896]{1,0:T(8,128)(2,1)S(1)} %bitcast.13, ...), custom_call_target="tpu_custom_call" | custom-call | tf_op jit(solution)/shard_map/pallas_call | solution.py:187
  47.8 70.4 %all-reduce.2 = (bf16[16,1024]{1,0:T(8,128)(2,1)S(1)}, bf16[16,1024]{1,0:T(8,128)(2,1)S(1)}, bf16[16,1024]{1,0:T(8,128)(2,1)S(1)}, bf16[16,1024]{1,0:T(8,128)(2,...) all-reduce(bf16[16,1024]{1,0:T(8,128)(2,1)S(1)} %get-tuple-element., ...), channel_id=1, replica_groups=mesh['node'=64,'local'=16] {'local'}, use_global_device_ids=true, to_apply=%region_0.0 | all-reduce | flops 1048576 | bytes 4194304 | tf_op jit(solution)/shard_map/psum | solution.py:235
  118.2 4.6 %shard_map.87 = bf16[512,1024]{1,0:T(8,128)(2,1)} custom-call(bf16[16,1024]{1,0:T(8,128)(2,1)S(1)} %get-tuple-element.147.refs_0_, bf16[16,1024]{1,0:T(8,128)(2,1)S(1)} %get-tuple-element.148.refs_1_, bf16[16,1024]{1,0:T(8,128)(2,1)S(1)} %get-tuple-element.149.refs_2_, bf16[16,1024]{1,0:T(8,128)(2,1)S(1)} %get-tuple-element.150.refs_3_, ...), custom_call_target="tpu_custom_call" | custom-call | tf_op jit(solution)/shard_map/pallas_call | solution.py:187
  122.8 0.0 copy-start
  122.8 0.0 copy-start.1
  122.8 19.5 %all-to-all-start.1 = ((bf16[64,8,1024]{2,1,0:T(8,128)(2,1)}), bf16[64,8,1024]{2,1,0:T(8,128)(2,1)S(1)}, u32[]{:S(2)}, u32[]{:S(2)}) async-start(bf16[64,8,1024]{2,1,0:T(8,128)(2,1)} %bitcast.7), calls=%async_computation.1 | async-start | bytes 2097152 | tf_op jit(solution)/shard_map/all_to_all | solution.py:214
  142.4 0.0 copy-done
  142.4 0.0 copy-done.1
  142.4 0.5 shard_map.88.stack_ref
  142.9 27.4 %all-to-all-done.1 = bf16[64,8,1024]{2,1,0:T(8,128)(2,1)S(1)} async-done(((bf16[64,8,1024]{2,1,0:T(8,128)(2,1)}), bf16[64,8,1024]{2,1,0:T(8,128)(2,1)S(1)}, u32[]{:S(2)}, u32[]{:S(2)}) %all-to-all-start.1) | async-done | bytes 1048608 | tf_op jit(solution)/shard_map/all_to_all | solution.py:214
  170.4 1.1 shard_map.89
Async XLA Ops:
  122.8 19.6 %copy-start = (s32[32,8]{0,1:T(8,128)S(1)}, s32[32,8]{0,1:T(8,128)}, u32[]{:S(2)}) copy-start(s32[32,8]{0,1:T(8,128)} %param.8) | copy-start | bytes 3076
  122.8 19.6 %copy-start.1 = (f32[32,8]{0,1:T(8,128)S(1)}, f32[32,8]{0,1:T(8,128)}, u32[]{:S(2)}) copy-start(f32[32,8]{0,1:T(8,128)} %param.9) | copy-start | bytes 3076
  122.8 47.5 %all-to-all-start.1 = ((bf16[64,8,1024]{2,1,0:T(8,128)(2,1)}), bf16[64,8,1024]{2,1,0:T(8,128)(2,1)S(1)}, u32[]{:S(2)}, u32[]{:S(2)}) async-start(bf16[64,8,1024]{2,1,0:T(8,128)(2,1)} %bitcast.7), calls=%async_computation.1 | async-start | bytes 2097152 | tf_op jit(solution)/shard_map/all_to_all | solution.py:214

commit v5 on v3

--- a/solution.py
+++ b/solution.py
@@ -217,6 +217,15 @@
         + [pltpu.VMEM((top, tok), jnp.int32), pltpu.SemaphoreType.DMA((3,))],
     )
     x_dy = exchange(sent)
+    late_routes, late_gates, x_dy = lax.optimization_barrier((routes_t, gate_probs.T, x_dy))
+    places = call(
+        functools.partial(places_kernel, nodes, capacity),
+        [VMEM] * 2,
+        jax.ShapeDtypeStruct(((3 + top) * tok, rows), BF16),
+        late_routes,
+        late_gates,
+    )
+    places, x_dy = lax.optimization_barrier((places, x_dy))
     terms = call(
         functools.partial(terms_kernel, parts),
         [VMEM, HBM, HBM],
@@ -235,14 +244,6 @@
         + [pltpu.VMEM((feat, hidden), BF16)] * 2
         + [pltpu.SemaphoreType.DMA((len(sums) + 2,))],
         limit=32,
-    )
-    late_routes, late_gates, back = lax.optimization_barrier((routes_t, gate_probs.T, back))
-    places = call(
-        functools.partial(places_kernel, nodes, capacity),
-        [VMEM] * 2,
-        jax.ShapeDtypeStruct(((3 + top) * tok, rows), BF16),
-        late_routes,
-        late_gates,
     )
     returned = exchange(back)
     mixed, d_tokens, d_gates = call(

time: 172 us -> 171 us (level)
  blocking collectives: 113 us -> 160 us
  waiting for transfers between devices: 27.4 us -> 0 us
  starting transfers between devices: 19.5 us -> 0 us
    all_to_all x1 -> x2, blocking collectives: 42.8 us -> 90.2 us  [exchange(): lax.all_to_all(values.reshape(nodes, capacity, values.shape[1]), 'node',...]
    all_to_all x1 -> x0, waiting for transfers between devices: 27.4 us -> none  [exchange(): lax.all_to_all(values.reshape(nodes, capacity, values.shape[1]), 'node',...]
    all_to_all x1 -> x0, starting transfers between devices: 19.5 us -> none  [exchange(): lax.all_to_all(values.reshape(nodes, capacity, values.shape[1]), 'node',...]
  transfers between devices with their start and end apart: 1 -> 0, of which waited for: 1 -> 0; matrix products, arithmetic and copies ran while one was open for 0% -> 0% of each run, Pallas kernels for 0% -> 0%
where the time goes in v5:
time: 171 us
  blocking collectives  160 us (94%)
  Pallas kernels  10.1 us (6%)
    all_to_all x2, blocking collectives, exchange(): lax.all_to_all(values.reshape(nodes, capacity, values.shape[1]), 'node',...  90.2 us
    psum x1, blocking collectives, body(): sums = lax.psum(tuple(terms), 'local')  70.1 us
    pallas_call x5, Pallas kernels, call(): pl.pallas_call(kernel, out_shape=out_shape, in_specs=in_specs, out_specs=...  10.1 us

profile of v5, /device:TPU:1, one launch (start us, length us, event | category | flops | bytes accessed | tf_op | source)
XLA Modules:
  0.0 171.1 jit_solution(16811245235130382617)
XLA Ops:
  0.6 1.7 shard_map.85
  2.3 0.0 copy-start
  2.4 0.0 copy-start.1
  2.4 42.8 %all_to_all.10 = bf16[64,8,896]{2,1,0:T(8,128)(2,1)S(1)} all-to-all(bf16[64,8,896]{2,1,0:T(8,128)(2,1)S(1)} %bitcast.13), channel_id=1, replica_groups=mesh['node'=64,'local'=16] {'node'}, dimensions={0} | all-to-all | bytes 1835008 | tf_op jit(solution)/shard_map/all_to_all | solution.py:207
  45.2 0.0 copy-done
  45.2 0.0 copy-done.1
  45.2 0.5 shard_map.86.stack_ref
  45.7 2.8 %shard_map.87 = (bf16[16,1024]{1,0:T(8,128)(2,1)S(1)}, bf16[16,1024]{1,0:T(8,128)(2,1)S(1)}, bf16[16,1024]{1,0:T(8,128)(2,1)S(1)}, bf16[16,1024]{1,0:T(8,128)(2,...) custom-call(bf16[512,896]{1,0:T(8,128)(2,1)S(1)} %bitcast.14, ...), custom_call_target="tpu_custom_call" | custom-call | tf_op jit(solution)/shard_map/pallas_call | solution.py:180
  48.5 70.1 %all-reduce.2 = (bf16[16,1024]{1,0:T(8,128)(2,1)}, bf16[16,1024]{1,0:T(8,128)(2,1)}, bf16[16,1024]{1,0:T(8,128)(2,1)}, bf16[16,1024]{1,0:T(8,128)(2,1)}, bf16[16...) all-reduce(bf16[16,1024]{1,0:T(8,128)(2,1)S(1)} %get-tuple-element., ...), channel_id=1, replica_groups=mesh['node'=64,'local'=16] {'local'}, use_global_device_ids=true, to_apply=%region_0.0 | all-reduce | flops 1048576 | bytes 4194304 | tf_op jit(solution)/shard_map/psum | solution.py:237
  118.7 3.9 %shard_map.88 = bf16[512,1024]{1,0:T(8,128)(2,1)S(1)} custom-call(bf16[16,1024]{1,0:T(8,128)(2,1)} %get-tuple-element.151.refs_0_, bf16[16,1024]{1,0:T(8,128)(2,1)} %get-tuple-element.152.refs_1_, bf16[16,1024]{1,0:T(8,128)(2,1)} %get-tuple-element.153.refs_2_, bf16[16,1024]{1,0:T(8,128)(2,1)} %get-tuple-element.154.refs_3_, ...), custom_call_target="tpu_custom_call" | custom-call | tf_op jit(solution)/shard_map/pallas_call | solution.py:180
  122.6 47.4 %all_to_all.11 = bf16[64,8,1024]{2,1,0:T(8,128)(2,1)S(1)} all-to-all(bf16[64,8,1024]{2,1,0:T(8,128)(2,1)S(1)} %bitcast.11), channel_id=1, replica_groups=mesh['node'=64,'local'=16] {'node'}, dimensions={0} | all-to-all | bytes 2097152 | tf_op jit(solution)/shard_map/all_to_all | solution.py:207
  170.0 1.1 shard_map.89
Async XLA Ops:
  2.3 42.8 %copy-start = (s32[32,8]{0,1:T(8,128)S(1)}, s32[32,8]{0,1:T(8,128)}, u32[]{:S(2)}) copy-start(s32[32,8]{0,1:T(8,128)} %param.8) | copy-start | bytes 3076
  2.4 42.8 %copy-start.1 = (f32[32,8]{0,1:T(8,128)S(1)}, f32[32,8]{0,1:T(8,128)}, u32[]{:S(2)}) copy-start(f32[32,8]{0,1:T(8,128)} %param.9) | copy-start | bytes 3076
